TPU v7x, 32 devices: a whole 2x2x4 slice. The times are simulated.
32 devices in a mesh: dp: 16 (over z, y, x), pipe: 2 (over core).
Axes of the slice: x: 2, y: 2, z: 4, core: 2. Of those that a mesh axis runs over, the one named last changes fastest.
Arguments:
- blocks: bfloat16 [2, 3072, 1024], P(None, 'dp'), may hold values from -6 to 6
- dest: int32 [2, 16, 48], replicated, may hold values from 0 to 15, as said below
- resets: int32 [2, 32], replicated, may hold values from 1 to 3071
- w_query: bfloat16 [4, 1024, 512], P('pipe'), may hold values from -0.1875 to 0.1875
- gain: float32 [4, 1024], P('pipe'), may hold values from 0.5 to 1.5
- decay: float32 [4, 8], P('pipe'), may hold values from 0 to 1
- cot: bfloat16 [2, 3072, 1024], P(None, 'dp'), may hold values from -0.076171875 to 0.076171875
Outputs:
- weight_grads: float32 [4, 1024, 512], P('pipe', 'dp')
Inputs may be any that keep to these rules, and one draw needn't show every extreme that they name: dest[m, i, j] = (i + o) mod 16 for an offset o that depends only on m and j, so each rank receives exactly one block j for every j; a rank sends at most 3 of its blocks to one rank, and exactly 3 to some rank.
All inputs are finite; a program needn't handle non-finite values.
Results may differ from a plain program's by a relative error of at most 0.018.
Values may be sent and summed in bfloat16 or wider, within the bound.
A program may use at most 64 MiB of HBM per device.

v0:
```python
import jax
import jax.numpy as jnp
from jax import lax
from jax.sharding import PartitionSpec as P

CH = 4


EPS = 1e-05


def shifted(x, axis, by):
    devices = lax.axis_size(axis)
    pairs = [(i, i + by) for i in range(devices) if 0 <= i + by < devices]
    return lax.ppermute(x, axis, pairs)


def shortened(x):

    def short(part):
        return part.astype(jnp.bfloat16) if part.dtype == jnp.float32 else part

    return jax.tree.map(short, x)


def normed_project(x, weight, gain, extra):
    x32 = x.astype(jnp.float32)
    scale = lax.rsqrt(jnp.mean(x32 * x32, axis=-1, keepdims=True) + EPS)
    z = (x32 * scale * gain).astype(jnp.bfloat16)
    q = (jnp.dot(z, weight, preferred_element_type=jnp.float32) + extra).astype(jnp.bfloat16)
    return (z, q)


def tables(log_rate, flags):
    count = jnp.cumsum(flags)
    index = jnp.arange(flags.shape[0]).astype(jnp.float32)
    diff = index[:, None] - index[None, :]
    same = (count[:, None] == count[None, :]) & (diff >= 0)
    return jnp.where(same[None], jnp.exp(diff[None] * log_rate[:, None, None]), 0.0)


def section_tables(log_rate, flags):
    length = flags.shape[0]
    intra = tables(log_rate.reshape(-1), flags)
    return intra.reshape(log_rate.shape[0], log_rate.shape[1], length, length)


def finish(x, heads_out):
    normal = heads_out * lax.rsqrt(jnp.mean(heads_out * heads_out, axis=-1, keepdims=True) + EPS)
    return (x.astype(jnp.float32) + normal.reshape(x.shape)).astype(jnp.bfloat16)


def local_layer(x, extra, weight, gain_row, intra):
    z, q = normed_project(x, weight, gain_row, extra)
    heads = intra.shape[0]
    length = x.shape[0]
    query_rows = q.astype(jnp.float32).reshape(length, heads, -1)
    value_rows = z.reshape(length, heads, -1)
    scores = jnp.einsum("thk,shk->hts", query_rows, query_rows) * intra
    mixing_weights = scores.astype(jnp.bfloat16)
    outputs = jnp.einsum(
        "hts,shv->thv", mixing_weights, value_rows, preferred_element_type=jnp.float32
    )
    return (finish(x, outputs), z)


def section(x, extras, weight, gain, intra):
    normals = []
    for depth in range(weight.shape[0]):
        x, z = local_layer(x, extras[depth], weight[depth], gain[depth], intra[depth])
        normals.append(z)
    return (x, jnp.stack(normals))


def local(blocks, dest, resets, w_query, gain, decay, cot):
    groups = lax.axis_size("dp")
    segments = lax.axis_size("pipe")
    rank = lax.axis_index("dp")
    segment = lax.axis_index("pipe")
    batches, rows, width = blocks.shape
    per_rank = rows // CH
    room = (per_rank + groups - 1) // groups
    mine = blocks.reshape(batches, per_rank, CH * width)
    own = lax.dynamic_index_in_dim(dest, rank, 1, keepdims=False)
    order = jnp.arange(per_rank)
    before_mask = order[None, :] < order[:, None]
    matching = own[:, :, None] == own[:, None, :]
    before = jnp.sum((matching & before_mask[None]).astype(jnp.int32), axis=2)
    target = own * room + before
    slot_ids = jnp.arange(groups * room, dtype=jnp.int32)
    send_map = (target[:, None, :] == slot_ids[None, :, None]).astype(jnp.bfloat16)
    outgoing = jnp.einsum(
        "mtj,mjc->mtc", send_map, mine, preferred_element_type=jnp.float32
    ).astype(jnp.bfloat16)
    incoming = lax.all_to_all(outgoing, "dp", split_axis=1, concat_axis=1, tiled=True)
    hits = (dest == rank).astype(jnp.int32)
    rank_in = jnp.cumsum(hits, axis=2) - 1
    senders = jnp.arange(groups, dtype=jnp.int32)[None, :, None]
    source = jnp.sum(hits * (senders * room + rank_in), axis=1)
    recv_map = (source[:, :, None] == slot_ids[None, None, :]).astype(jnp.bfloat16)
    packed = (
        jnp.einsum("mjt,mtc->mjc", recv_map, incoming, preferred_element_type=jnp.float32)
        .astype(jnp.bfloat16)
        .reshape(batches, rows, width)
    )
    positions = rank * rows + jnp.arange(rows, dtype=jnp.int32)
    flags = jnp.any(positions[None, :, None] == resets[:, None, :], axis=-1).astype(jnp.float32)
    layers = w_query.shape[0]
    hidden_qk = w_query.shape[2]
    log_rate = jnp.log(decay)
    zero_extra = jnp.zeros((layers, rows, hidden_qk), jnp.float32)
    zero_rows = jnp.zeros((rows, width), jnp.bfloat16)
    ticks = batches + segments - 1

    def forward_tick(tick, carry):
        inbox, saved_x = carry
        batch = tick - segment
        valid = (batch >= 0) & (batch < batches)
        pick = jnp.clip(batch, 0, batches - 1)
        x_in = jnp.where(
            segment == 0, lax.dynamic_index_in_dim(packed, pick, 0, keepdims=False), inbox
        )
        flag_row = lax.dynamic_index_in_dim(flags, pick, 0, keepdims=False)

        def forward_active(x):
            intra = section_tables(log_rate, flag_row)
            return section(x, zero_extra, w_query, gain, intra)[0]

        def forward_resting(x):
            return zero_rows

        output = lax.cond(valid, forward_active, forward_resting, x_in)
        keep_x = jnp.where(valid, x_in, lax.dynamic_index_in_dim(saved_x, pick, 0, keepdims=False))
        saved_x = lax.dynamic_update_index_in_dim(saved_x, keep_x, pick, 0)
        inbox = shifted(output, "pipe", 1)
        return (inbox, saved_x)

    start = (zero_rows, jnp.zeros((batches, rows, width), jnp.bfloat16))
    _, saved_x = lax.fori_loop(0, ticks, forward_tick, start)

    def backward_tick(tick, carry):
        inbox, grad_total = carry
        batch = tick - (segments - 1 - segment)
        valid = (batch >= 0) & (batch < batches)
        pick = jnp.clip(batch, 0, batches - 1)
        upstream = jnp.where(
            segment == segments - 1, lax.dynamic_index_in_dim(cot, pick, 0, keepdims=False), inbox
        )
        x_in = lax.dynamic_index_in_dim(saved_x, pick, 0, keepdims=False)
        flag_row = lax.dynamic_index_in_dim(flags, pick, 0, keepdims=False)

        def backward_active(args):
            x, d_out = args
            intra = section_tables(log_rate, flag_row)

            def mixing(x_arg, e_arg):
                return section(x_arg, e_arg, w_query, gain, intra)

            _, pullback, normal_rows = jax.vjp(mixing, x, zero_extra, has_aux=True)
            d_input, d_extra = pullback(d_out)
            d_weight = jnp.einsum(
                "ltd,ltk->ldk",
                normal_rows,
                d_extra.astype(jnp.bfloat16),
                preferred_element_type=jnp.float32,
            )
            return (d_input, d_weight)

        def backward_resting(args):
            return (zero_rows, jnp.zeros((layers, width, hidden_qk), jnp.float32))

        d_x, d_weight = lax.cond(valid, backward_active, backward_resting, (x_in, upstream))
        inbox = jax.tree.map(
            lambda part, own: part.astype(own.dtype), shifted(shortened(d_x), "pipe", -1), d_x
        )
        return (inbox, grad_total + d_weight)

    grad_start = (zero_rows, jnp.zeros((layers, width, hidden_qk), jnp.float32))
    _, grad_total = lax.fori_loop(0, ticks, backward_tick, grad_start)
    full = lax.psum(grad_total, "dp")
    share = width // groups
    own_rows = lax.dynamic_slice_in_dim(full, rank * share, share, 1)
    return own_rows


def solution(mesh):
    placed = (
        P(None, "dp", None),
        P(),
        P(),
        P("pipe", None, None),
        P("pipe", None),
        P("pipe", None),
        P(None, "dp", None),
    )
    return jax.shard_map(
        local, mesh=mesh, in_specs=placed, out_specs=P("pipe", "dp", None), check_vma=False
    )
```

profile of v0, /device:TPU:1, one launch (start us, length us, event | category | flops | bytes accessed | tf_op | source)
XLA Modules:
  0.0 477.5 jit_solution(12278367867636024328)
XLA Ops:
  11.1 7.4 %all-to-all-start = ((bf16[2,48,4096]{2,0,1:T(2,128)(2,1)}), bf16[2,48,4096]{2,0,1:T(2,128)(2,1)S(1)}, u32[]{:S(2)}, u32[]{:S(2)}) async-start(bf16[2,48,4096]{2,0,1:T(2,128)(2,1)} %copy.101), calls=%async_computation | async-start | bytes 1572864 | tf_op jit(solution)/shard_map/all_to_all | solution.py:95
  20.4 15.4 %all-to-all-done = bf16[2,48,4096]{2,0,1:T(2,128)(2,1)S(1)} async-done(((bf16[2,48,4096]{2,0,1:T(2,128)(2,1)}), bf16[2,48,4096]{2,0,1:T(2,128)(2,1)S(1)}, u32[]{:S(2)}, u32[]{:S(2)}) %all-to-all-start) | async-done | bytes 786464 | tf_op jit(solution)/shard_map/all_to_all | solution.py:95
  39.3 89.7 %while.34 = (s32[]{:T(128)}, bf16[192,1024]{1,0:T(8,128)(2,1)S(1)}, bf16[2,192,1024]{2,1,0:T(8,128)(2,1)}, s32[]{:T(128)}, pred[]{:T(512)}, /*index=5*/bf16[2,19...) while((s32[]{:T(128)}, bf16[192,1024]{1,0:T(8,128)(2,1)S(1)}, ...), condition=%wide.region_13.14_spmd, body=%wide.region_4.13_spmd.sunk | while | flops 639000128 | bytes 24460156 | solution.py:139
  44.5 26.3 %collective-permute-done = bf16[192,1024]{1,0:T(8,128)(2,1)S(1)} collective-permute-done((bf16[192,1024]{1,0:T(8,128)(2,1)}, bf16[192,1024]{1,0:T(8,128)(2,1)S(1)}, u32[]{:S(2)}, u32[]{:S(2)}) %collective-permute-start) | collective-permute-done | bytes 393248 | tf_op jit(solution)/shard_map/while/body/eval_jaxpr/ppermute | solution.py:15
  73.8 22.3 %conditional.5 = (bf16[192,1024]{1,0:T(8,128)(2,1)}) conditional(s32[]{:T(128)} %convert_element_type.590, () %tuple.110, (bf16[192,1024]{1,0:T(8,128)(2,1)S(1)}, f32[2,1024]{1,0:T(2,128)}, bf16[2,1024,512]{2,1,0:T(8,128)(2,1)}, f32[2,192]{1,0:T(2,128)}, s32[]{:T(128)}, /*index=5*/f32[2,8]{1,0:T(2,128)}) %tuple.111), branch_computations={%region_5.5_spmd, %region_6.12_spmd} | conditional | flops 638606912 | bytes 20133476 | solution.py:132
  82.2 2.6 multiply_reduce_fusion.1
  87.1 2.3 convolution_convert_fusion
  91.2 2.7 multiply_reduce_fusion
  93.9 2.2 fusion.17
  97.4 2.5 collective-permute-done
  102.9 22.3 %conditional.5 = (bf16[192,1024]{1,0:T(8,128)(2,1)}) conditional(s32[]{:T(128)} %convert_element_type.590, () %tuple.110, (bf16[192,1024]{1,0:T(8,128)(2,1)S(1)}, f32[2,1024]{1,0:T(2,128)}, bf16[2,1024,512]{2,1,0:T(8,128)(2,1)}, f32[2,192]{1,0:T(2,128)}, s32[]{:T(128)}, /*index=5*/f32[2,8]{1,0:T(2,128)}) %tuple.111), branch_computations={%region_5.5_spmd, %region_6.12_spmd} | conditional | flops 638606912 | bytes 20133476 | solution.py:132
  111.3 2.6 multiply_reduce_fusion.1
  116.2 2.3 convolution_convert_fusion
  120.3 2.7 multiply_reduce_fusion
  123.0 2.2 fusion.17
  126.5 2.5 collective-permute-done
  129.1 172.7 %while.35 = (s32[]{:T(128)}, bf16[192,1024]{1,0:T(8,128)(2,1)S(1)}, f32[2,1024,512]{2,1,0:T(8,128)}, s32[]{:T(128)}, pred[]{:T(512)}, /*index=5*/bf16[2,192,1024...) while((s32[]{:T(128)}, bf16[192,1024]{1,0:T(8,128)(2,1)S(1)}, ...), condition=%wide.region_27.28_spmd.clone, body=%wide.region_14.27_spmd.clone.sunk | while | flops 1917687168 | bytes 125535752 | solution.py:179
  129.3 51.1 %conditional.6 = (bf16[192,1024]{1,0:T(8,128)(2,1)}, f32[2,1024,512]{2,1,0:T(8,128)}) conditional(s32[]{:T(128)} %convert_element_type.591, () %tuple.113, (pred[]{:T(512)}, s32[]{:T(128)}, bf16[2,192,1024]{2,1,0:T(8,128)(2,1)}, bf16[192,1024]{1,0:T(8,128)(2,1)S(1)}, bf16[2,192,1024]{2,1,0:T(8,128)(2,1)}, /*index=5*/f32[2,1024]{1,0:T(2,128)}, ...), branch_computations={%region_15.15_spmd, %region_16.0_spmd} | conditional | flops 1915590016 | bytes 111379688 | solution.py:172
  148.1 2.1 reshape.555
  153.1 2.4 convolution_convert_fusion.8
  171.5 3.8 fusion.64
  181.7 5.1 %select_add_fusion.2 = f32[2,1024,512]{2,1,0:T(8,128)} fusion(f32[2,1024,512]{2,1,0:T(8,128)} %get-tuple-element.814, f32[2,1024,512]{2,1,0:T(8,128)} %get-tuple-element.874, pred[]{:T(512)S(6)} %compare.7), kind=kLoop, calls=%fused_computation.171.clone.1 | loop fusion | flops 2097152 | bytes 12582913 | tf_op jit(solution)/shard_map/while/body/eval_jaxpr/add | solution.py:176
  186.8 51.0 %conditional.6 = (bf16[192,1024]{1,0:T(8,128)(2,1)}, f32[2,1024,512]{2,1,0:T(8,128)}) conditional(s32[]{:T(128)} %convert_element_type.591, () %tuple.113, (pred[]{:T(512)}, s32[]{:T(128)}, bf16[2,192,1024]{2,1,0:T(8,128)(2,1)}, bf16[192,1024]{1,0:T(8,128)(2,1)S(1)}, bf16[2,192,1024]{2,1,0:T(8,128)(2,1)}, /*index=5*/f32[2,1024]{1,0:T(2,128)}, ...), branch_computations={%region_15.15_spmd, %region_16.0_spmd} | conditional | flops 1915590016 | bytes 111379688 | solution.py:172
  205.6 2.1 reshape.555
  210.6 2.4 convolution_convert_fusion.8
  229.0 3.8 fusion.64
  239.2 6.4 %select_add_fusion.2 = f32[2,1024,512]{2,1,0:T(8,128)} fusion(f32[2,1024,512]{2,1,0:T(8,128)} %get-tuple-element.814, f32[2,1024,512]{2,1,0:T(8,128)} %get-tuple-element.874, pred[]{:T(512)S(6)} %compare.7), kind=kLoop, calls=%fused_computation.171.clone.1 | loop fusion | flops 2097152 | bytes 12582913 | tf_op jit(solution)/shard_map/while/body/eval_jaxpr/add | solution.py:176
  245.6 3.3 conditional.6
  245.6 2.5 broadcast.419
  248.9 46.3 %collective-permute-start.1 = (bf16[192,1024]{1,0:T(8,128)(2,1)}, bf16[192,1024]{1,0:T(8,128)(2,1)S(1)}, u32[]{:S(2)}, u32[]{:S(2)}) collective-permute-start(bf16[192,1024]{1,0:T(8,128)(2,1)} %get-tuple-element.813), channel_id=1, source_target_pairs={{1,0},{3,2},{5,4},{7,6},{9,8},{11,10},{13,12},{15,14},{17,16},{19,... | collective-permute-start | bytes 1179656 | tf_op jit(solution)/shard_map/while/body/eval_jaxpr/ppermute | solution.py:15
  295.3 6.4 %select_add_fusion.2 = f32[2,1024,512]{2,1,0:T(8,128)} fusion(f32[2,1024,512]{2,1,0:T(8,128)} %get-tuple-element.814, f32[2,1024,512]{2,1,0:T(8,128)} %get-tuple-element.874, pred[]{:T(512)S(6)} %compare.7), kind=kLoop, calls=%fused_computation.171.clone.1 | loop fusion | flops 2097152 | bytes 12582913 | tf_op jit(solution)/shard_map/while/body/eval_jaxpr/add | solution.py:176
  301.8 167.2 %all-reduce.6.cloned.1.call-done = f32[2,1024,512]{2,1,0:T(8,128)} async-done(((f32[2,1024,512]{2,1,0:T(8,128)}), f32[2,1024,512]{2,1,0:T(8,128)}) %all-reduce.6.cloned.1.call-update) | async-done | bytes 4194320 | tf_op jit(solution)/shard_map/psum | solution.py:180
  (327 shorter events, 138.7 us)
Async XLA Ops:
  6.5 12.1 %copy-start.34 = (s32[2,16,48]{2,1,0:T(8,128)S(1)}, s32[2,16,48]{2,1,0:T(8,128)}, u32[]{:S(2)}) copy-start(s32[2,16,48]{2,1,0:T(8,128)} %param.16) | copy-start | bytes 18436
  6.6 12.5 %copy-start.35 = (s32[2,32]{1,0:T(2,128)S(1)}, s32[2,32]{1,0:T(2,128)}, u32[]{:S(2)}) copy-start(s32[2,32]{1,0:T(2,128)} %param.17) | copy-start | bytes 772
  6.6 13.2 %copy-start.36 = (f32[2,8]{1,0:T(2,128)S(1)}, f32[2,8]{1,0:T(2,128)}, u32[]{:S(2)}) copy-start(f32[2,8]{1,0:T(2,128)} %param.20) | copy-start | bytes 196
  11.1 24.7 %all-to-all-start = ((bf16[2,48,4096]{2,0,1:T(2,128)(2,1)}), bf16[2,48,4096]{2,0,1:T(2,128)(2,1)S(1)}, u32[]{:S(2)}, u32[]{:S(2)}) async-start(bf16[2,48,4096]{2,0,1:T(2,128)(2,1)} %copy.101), calls=%async_computation | async-start | bytes 1572864 | tf_op jit(solution)/shard_map/all_to_all | solution.py:95
  18.5 450.5 %all-reduce.6.cloned.1.call-start = ((), (), s32[]{:S(2)}) async-start(), calls=%async_computation.1 | async-start | bytes 8388608 | tf_op jit(solution)/shard_map/psum | solution.py:180
  43.2 27.6 %collective-permute-start = (bf16[192,1024]{1,0:T(8,128)(2,1)}, bf16[192,1024]{1,0:T(8,128)(2,1)S(1)}, u32[]{:S(2)}, u32[]{:S(2)}) collective-permute-start(bf16[192,1024]{1,0:T(8,128)(2,1)} %get-tuple-element.900), channel_id=1, source_target_pairs={{0,1},{2,3},{4,5},{6,7},{8,9},{10,11},{12,13},{14,15},{16,17},{18,... | collective-permute-start | bytes 1179656 | tf_op jit(solution)/shard_map/while/body/eval_jaxpr/ppermute | solution.py:15
  74.0 6.1 %copy-start.33 = (f32[192]{0:T(256)}, f32[192]{0:T(256)S(1)}, u32[]{:S(2)}) copy-start(f32[192]{0:T(256)S(1)} %add_rsqrt_fusion.3) | copy-start | bytes 2308 | tf_op jit(solution)/shard_map/while/body/eval_jaxpr/cond
  89.4 4.5 copy-start.14
  96.1 3.8 collective-permute-start
  103.1 6.1 %copy-start.33 = (f32[192]{0:T(256)}, f32[192]{0:T(256)S(1)}, u32[]{:S(2)}) copy-start(f32[192]{0:T(256)S(1)} %add_rsqrt_fusion.3) | copy-start | bytes 2308 | tf_op jit(solution)/shard_map/while/body/eval_jaxpr/cond
  118.5 4.5 copy-start.14
  125.2 3.8 collective-permute-start
  130.5 12.1 %copy-start.28 = (f32[192]{0:T(256)}, f32[192]{0:T(256)S(1)}, u32[]{:S(2)}) copy-start(f32[192]{0:T(256)S(1)} %fusion.84) | copy-start | bytes 2308 | tf_op jit(solution)/shard_map/while/body/eval_jaxpr/cond
  131.3 11.3 %copy-start.26 = (f32[1,1024]{1,0:T(1,128)}, f32[1,1024]{1,0:T(1,128)S(1)}, u32[]{:S(2)}) copy-start(f32[1,1024]{1,0:T(1,128)S(1)} %get-tuple-element.670) | copy-start | bytes 12292 | tf_op jit(solution)/shard_map/while/body/eval_jaxpr/cond
  163.3 4.3 copy-start.1
  170.1 5.2 %copy-start.2 = (f32[192,8,128]{2,0,1:T(8,128)S(1)}, f32[192,8,128]{2,0,1:T(8,128)}, u32[]{:S(2)}) copy-start(f32[192,8,128]{2,0,1:T(8,128)} %copy-done) | copy-start | bytes 2359300 | tf_op jit(solution)/shard_map/while/body/eval_jaxpr/cond
  170.1 5.2 %copy-start.6 = (f32[24,8,8,128]{3,2,1,0:T(8,128)S(1)}, f32[24,8,8,128]{3,2,1,0:T(8,128)}, u32[]{:S(2)}) copy-start(f32[24,8,8,128]{3,2,1,0:T(8,128)} %copy-done.5) | copy-start | bytes 2359300 | tf_op jit(solution)/shard_map/while/body/eval_jaxpr/cond
  170.1 5.2 %copy-start.8 = (bf16[8,192,192]{2,1,0:T(8,128)(2,1)S(1)}, bf16[8,192,192]{2,1,0:T(8,128)(2,1)}, u32[]{:S(2)}) copy-start(bf16[8,192,192]{2,1,0:T(8,128)(2,1)} %copy-done.7) | copy-start | bytes 1769476 | tf_op jit(solution)/shard_map/while/body/eval_jaxpr/cond
  171.4 4.8 %copy-start.23 = (bf16[8,192,64]{1,2,0:T(8,128)(2,1)S(1)}, bf16[8,192,64]{1,2,0:T(8,128)(2,1)}, u32[]{:S(2)}) copy-start(bf16[8,192,64]{1,2,0:T(8,128)(2,1)} %fusion.31) | copy-start | bytes 589828 | tf_op jit(solution)/shard_map/while/body/eval_jaxpr/cond
  171.5 4.8 %copy-start.27 = (f32[1,1024]{1,0:T(1,128)S(1)}, f32[1,1024]{1,0:T(1,128)}, u32[]{:S(2)}) copy-start(f32[1,1024]{1,0:T(1,128)} %copy-done.26) | copy-start | bytes 12292 | tf_op jit(solution)/shard_map/while/body/eval_jaxpr/cond
  180.3 6.5 %collective-permute-start.1 = (bf16[192,1024]{1,0:T(8,128)(2,1)}, bf16[192,1024]{1,0:T(8,128)(2,1)S(1)}, u32[]{:S(2)}, u32[]{:S(2)}) collective-permute-start(bf16[192,1024]{1,0:T(8,128)(2,1)} %get-tuple-element.813), channel_id=1, source_target_pairs={{1,0},{3,2},{5,4},{7,6},{9,8},{11,10},{13,12},{15,14},{17,16},{19,... | collective-permute-start | bytes 1179656 | tf_op jit(solution)/shard_map/while/body/eval_jaxpr/ppermute | solution.py:15
  188.0 12.1 %copy-start.28 = (f32[192]{0:T(256)}, f32[192]{0:T(256)S(1)}, u32[]{:S(2)}) copy-start(f32[192]{0:T(256)S(1)} %fusion.84) | copy-start | bytes 2308 | tf_op jit(solution)/shard_map/while/body/eval_jaxpr/cond
  188.8 11.3 %copy-start.26 = (f32[1,1024]{1,0:T(1,128)}, f32[1,1024]{1,0:T(1,128)S(1)}, u32[]{:S(2)}) copy-start(f32[1,1024]{1,0:T(1,128)S(1)} %get-tuple-element.670) | copy-start | bytes 12292 | tf_op jit(solution)/shard_map/while/body/eval_jaxpr/cond
  214.8 3.6 copy-start.17
  220.8 4.3 copy-start.1
  227.6 5.2 %copy-start.2 = (f32[192,8,128]{2,0,1:T(8,128)S(1)}, f32[192,8,128]{2,0,1:T(8,128)}, u32[]{:S(2)}) copy-start(f32[192,8,128]{2,0,1:T(8,128)} %copy-done) | copy-start | bytes 2359300 | tf_op jit(solution)/shard_map/while/body/eval_jaxpr/cond
  227.6 5.2 %copy-start.6 = (f32[24,8,8,128]{3,2,1,0:T(8,128)S(1)}, f32[24,8,8,128]{3,2,1,0:T(8,128)}, u32[]{:S(2)}) copy-start(f32[24,8,8,128]{3,2,1,0:T(8,128)} %copy-done.5) | copy-start | bytes 2359300 | tf_op jit(solution)/shard_map/while/body/eval_jaxpr/cond
  227.6 5.2 %copy-start.8 = (bf16[8,192,192]{2,1,0:T(8,128)(2,1)S(1)}, bf16[8,192,192]{2,1,0:T(8,128)(2,1)}, u32[]{:S(2)}) copy-start(bf16[8,192,192]{2,1,0:T(8,128)(2,1)} %copy-done.7) | copy-start | bytes 1769476 | tf_op jit(solution)/shard_map/while/body/eval_jaxpr/cond
  229.0 4.8 %copy-start.23 = (bf16[8,192,64]{1,2,0:T(8,128)(2,1)S(1)}, bf16[8,192,64]{1,2,0:T(8,128)(2,1)}, u32[]{:S(2)}) copy-start(bf16[8,192,64]{1,2,0:T(8,128)(2,1)} %fusion.31) | copy-start | bytes 589828 | tf_op jit(solution)/shard_map/while/body/eval_jaxpr/cond
  229.0 4.8 %copy-start.27 = (f32[1,1024]{1,0:T(1,128)S(1)}, f32[1,1024]{1,0:T(1,128)}, u32[]{:S(2)}) copy-start(f32[1,1024]{1,0:T(1,128)} %copy-done.26) | copy-start | bytes 12292 | tf_op jit(solution)/shard_map/while/body/eval_jaxpr/cond
  237.9 7.7 %collective-permute-start.1 = (bf16[192,1024]{1,0:T(8,128)(2,1)}, bf16[192,1024]{1,0:T(8,128)(2,1)S(1)}, u32[]{:S(2)}, u32[]{:S(2)}) collective-permute-start(bf16[192,1024]{1,0:T(8,128)(2,1)} %get-tuple-element.813), channel_id=1, source_target_pairs={{1,0},{3,2},{5,4},{7,6},{9,8},{11,10},{13,12},{15,14},{17,16},{19,... | collective-permute-start | bytes 1179656 | tf_op jit(solution)/shard_map/while/body/eval_jaxpr/ppermute | solution.py:15
  248.9 52.8 %collective-permute-start.1 = (bf16[192,1024]{1,0:T(8,128)(2,1)}, bf16[192,1024]{1,0:T(8,128)(2,1)S(1)}, u32[]{:S(2)}, u32[]{:S(2)}) collective-permute-start(bf16[192,1024]{1,0:T(8,128)(2,1)} %get-tuple-element.813), channel_id=1, source_target_pairs={{1,0},{3,2},{5,4},{7,6},{9,8},{11,10},{13,12},{15,14},{17,16},{19,... | collective-permute-start | bytes 1179656 | tf_op jit(solution)/shard_map/while/body/eval_jaxpr/ppermute | solution.py:15
  (47 other events, 89.7 us)
Sparse Core Ops, SparseCore 0:
  301.9 167.0 all-reduce.5
where the time goes:
time: 481 us; the launch traced here: 478 us
  waiting for transfers between devices  214 us (44%)
  other arithmetic  72.5 us (15%)
  matrix products  63.1 us (13%)
  starting transfers between devices  60.2 us (13%)
  local copies, waits for them, and re-layouts  52.6 us (11%)
  between operations  13.5 us (3%)
    psum x1, waiting for transfers between devices, local(): full = lax.psum(grad_total, 'dp')  167 us
    ppermute x6, starting transfers between devices, shifted(): return lax.ppermute(x, axis, pairs)  52.8 us
    ppermute x6, waiting for transfers between devices, shifted(): return lax.ppermute(x, axis, pairs)  31.4 us
    dot_general x12, matrix products, normed_project(): jnp.dot(z, weight, preferred_element_type=jnp.float32) + extra  24.1 us
    dot_general x16, matrix products, local_layer(): jnp.einsum('hts,shv->thv', mixing_weights, value_rows, preferred_element_...  22.1 us
    add x3, other arithmetic, backward_tick(): return (inbox, grad_total + d_weight)  18 us
    all_to_all x1, waiting for transfers between devices, local(): lax.all_to_all(outgoing, 'dp', split_axis=1, concat_axis=1, tiled=True)  15.4 us
    convert_element_type x12, local copies, waits for them, and re-layouts, normed_project(): (jnp.dot(z, weight, preferred_element_type=jnp.float32) + extra).astype(j...  13.3 us
  transfers between devices with their start and end apart: 8, of which 5 were waited for; matrix products, arithmetic and copies ran while one was open for 4% of the time, Pallas kernels for 0%

commit v1 on v0

--- a/solution.py
+++ b/solution.py
@@ -1,6 +1,10 @@
+import functools
+
 import jax
 import jax.numpy as jnp
 from jax import lax
+from jax.experimental import pallas as pl
+from jax.experimental.pallas import tpu as pltpu
 from jax.sharding import PartitionSpec as P
 
 CH = 4
@@ -72,7 +76,7 @@
     return (x, jnp.stack(normals))
 
 
-def local(blocks, dest, resets, w_query, gain, decay, cot):
+def pipelined(blocks, dest, resets, w_query, gain, decay, cot):
     groups = lax.axis_size("dp")
     segments = lax.axis_size("pipe")
     rank = lax.axis_index("dp")
@@ -183,6 +187,385 @@
     return own_rows
 
 
+MESH = pl.DeviceIdType.MESH
+F32 = jnp.float32
+BF16 = jnp.bfloat16
+
+
+def dot(a, b, ca=1, cb=0):
+    return lax.dot_general(a, b, (((ca,), (cb,)), ((), ())), preferred_element_type=F32)
+
+
+def iota(shape, dim):
+    return lax.broadcasted_iota(jnp.int32, shape, dim)
+
+
+def as_column(row):
+    n = row.shape[1]
+    eye = iota((n, n), 0) == iota((n, n), 1)
+    return jnp.sum(jnp.where(eye, jnp.broadcast_to(row, (n, n)), 0), axis=1, keepdims=True)
+
+
+def exchange_kernel(
+    groups, slot, blocks_ref, dest_ref, w_ref, gain_ref, decay_ref,
+    recv_ref, w_all, gain_all, decay_all, out_s, send_sem, recv_sem, par_send, par_recv, own_sem,
+):
+    me = lax.axis_index("dp")
+    core = lax.axis_index("pipe")
+    barrier = pltpu.get_barrier_semaphore()
+
+    def greet(k, carry):
+        pl.semaphore_signal(
+            barrier, inc=1, device_id=(lax.rem(me + k, groups), core), device_id_type=MESH
+        )
+        return carry
+
+    lax.fori_loop(1, groups, greet, 0)
+    pl.semaphore_signal(barrier, inc=1, device_id=(me, 1 - core), device_id_type=MESH)
+
+    own_copies = []
+    for i, (src, dst) in enumerate(((w_ref, w_all), (gain_ref, gain_all), (decay_ref, decay_all))):
+        own = pltpu.make_async_copy(src, dst.at[core], own_sem.at[i])
+        own.start()
+        own_copies.append(own)
+
+    rows = blocks_ref.shape[1]
+    per_rank = rows // CH
+    total = groups * slot
+    own_row = dest_ref[core, pl.ds(me, 1), :]
+    own_col = as_column(own_row)
+    order = (per_rank, per_rank)
+    earlier = (own_row == own_col) & (iota(order, 1) < iota(order, 0))
+    before = jnp.sum(jnp.where(earlier, 1, 0), axis=1, keepdims=True)
+    target = own_col * slot + before * CH
+    wide = (per_rank, rows)
+    spread = iota(wide, 1) // CH == iota(wide, 0)
+    target_row = jnp.sum(jnp.where(spread, jnp.broadcast_to(target, wide), 0), axis=0, keepdims=True)
+    target_row = target_row + iota((1, rows), 1) % CH
+    send_map = jnp.where(iota((total, rows), 0) == target_row, 1.0, 0.0).astype(BF16)
+    picked = dot(send_map, blocks_ref[core]).astype(BF16)
+    out_s[...] = picked.reshape(out_s.shape)
+
+    pl.semaphore_wait(barrier, groups)
+
+    def pair_copy(k):
+        there = lax.rem(me + k, groups)
+        return pltpu.make_async_remote_copy(
+            src_ref=out_s.at[there], dst_ref=recv_ref.at[me],
+            send_sem=send_sem.at[k], recv_sem=recv_sem.at[k],
+            device_id=(there, core), device_id_type=MESH,
+        )
+
+    def send(k, carry):
+        pair_copy(k).start()
+        return carry
+
+    lax.fori_loop(1, groups, send, 0)
+    part_copies = []
+    for i, (src, dst) in enumerate(((w_ref, w_all), (gain_ref, gain_all), (decay_ref, decay_all))):
+        part = pltpu.make_async_remote_copy(
+            src_ref=src, dst_ref=dst.at[core], send_sem=par_send.at[i], recv_sem=par_recv.at[i],
+            device_id=(me, 1 - core), device_id_type=MESH,
+        )
+        part.start()
+        part_copies.append(part)
+    recv_ref[me] = out_s[me]
+    for own in own_copies:
+        own.wait()
+
+    def arrive(k, carry):
+        pair_copy(k).wait()
+        return carry
+
+    lax.fori_loop(1, groups, arrive, 0)
+    for part in part_copies:
+        part.wait()
+
+
+def layers_kernel(
+    heads, slot, recv_ref, dest_ref, resets_ref, w_ref, gain_ref, decay_ref, cot_ref,
+    z_ref, g_ref, q_s, x_s, a_s, table_s, n_s, ro_s, r_s, dy_s, dv_s,
+):
+    me = lax.axis_index("dp")
+    core = lax.axis_index("pipe")
+    layers, rows, width = z_ref.shape
+    depth = w_ref.shape[1]
+    dk = g_ref.shape[2] // heads
+    dv = width // heads
+    per_rank = rows // CH
+    groups = dest_ref.shape[1]
+
+    hits = jnp.where(dest_ref[core] == me, 1.0, 0.0)
+    order = (per_rank, per_rank)
+    upper = jnp.where(iota(order, 0) < iota(order, 1), 1.0, 0.0).astype(BF16)
+    before = dot(hits.astype(BF16), upper)
+    sender = iota((groups, per_rank), 0).astype(F32)
+    source = jnp.sum(hits * (sender * slot + before * CH), axis=0, keepdims=True)
+    tall = (rows, per_rank)
+    spread = iota(tall, 0) // CH == iota(tall, 1)
+    source_col = jnp.sum(jnp.where(spread, jnp.broadcast_to(source, tall), 0.0), axis=1, keepdims=True)
+    source_col = source_col.astype(jnp.int32) + iota((rows, 1), 0) % CH
+    recv_map = jnp.where(iota((rows, groups * slot), 1) == source_col, 1.0, 0.0).astype(BF16)
+    x_s[0] = dot(recv_map, recv_ref[...].reshape(groups * slot, width)).astype(BF16)
+
+    resets = resets_ref[pl.ds(core, 1), :]
+    n_resets = resets.shape[1]
+    start = me * rows
+    count_col = jnp.sum(
+        jnp.where(resets <= iota((rows, n_resets), 0) + start, 1, 0), axis=1, keepdims=True
+    )
+    count_row = jnp.sum(
+        jnp.where(as_column(resets) <= iota((n_resets, rows), 1) + start, 1, 0), axis=0, keepdims=True
+    )
+    square = (rows, rows)
+    steps = iota(square, 0) - iota(square, 1)
+    same = (count_col == count_row) & (steps >= 0)
+    diff = steps.astype(F32)
+
+    def forward(l, carry):
+        x32 = x_s[l].astype(F32)
+        scale = lax.rsqrt(jnp.mean(x32 * x32, axis=1, keepdims=True) + EPS)
+        r_s[l] = scale
+        gain = gain_ref[l // depth, pl.ds(l % depth, 1), :]
+        z = (x32 * scale * gain).astype(BF16)
+        z_ref[l] = z
+        q = dot(z, w_ref[l // depth, l % depth]).astype(BF16)
+        q_s[l] = q
+        rates = jnp.log(decay_ref[l // depth, pl.ds(l % depth, 1), :])
+        for h in range(heads):
+            table = jnp.where(same, jnp.exp(diff * rates[:, h : h + 1]), 0.0)
+            table_s[l, h] = table
+            qh = q[:, h * dk : (h + 1) * dk]
+            a = (dot(qh, qh, 1, 1) * table).astype(BF16)
+            a_s[l, h] = a
+            cols = slice(h * dv, (h + 1) * dv)
+            o = dot(a, z[:, cols])
+            ro = lax.rsqrt(jnp.mean(o * o, axis=1, keepdims=True) + EPS)
+            n = o * ro
+            n_s[l, :, cols] = n
+            ro_s[l, h] = ro
+            x_s[l + 1, :, cols] = (x32[:, cols] + n).astype(BF16)
+        return carry
+
+    lax.fori_loop(0, layers, forward, 0)
+    dy_s[...] = cot_ref[core]
+
+    def backward(i, carry):
+        l = layers - 1 - i
+        for h in range(heads):
+            cols = slice(h * dv, (h + 1) * dv)
+            dn = dy_s[:, cols].astype(F32)
+            n = n_s[l, :, cols]
+            do = ro_s[l, h] * (dn - n * jnp.mean(dn * n, axis=1, keepdims=True))
+            do = do.astype(BF16)
+            da = dot(do, z_ref[l, :, cols], 1, 1)
+            ds = (da * table_s[l, h]).astype(BF16)
+            dv_s[:, cols] = dot(a_s[l, h], do, 0, 0)
+            qh = q_s[l, :, h * dk : (h + 1) * dk]
+            g_ref[l, :, h * dk : (h + 1) * dk] = (dot(ds, qh) + dot(ds, qh, 0, 0)).astype(BF16)
+
+        @pl.when(l > 0)
+        def _():
+            dz = dot(g_ref[l], w_ref[l // depth, l % depth], 1, 1) + dv_s[...]
+            gain = gain_ref[l // depth, pl.ds(l % depth, 1), :]
+            scale = r_s[l]
+            unit = x_s[l].astype(F32) * scale
+            dzg = dz * gain
+            dx = scale * (dzg - unit * jnp.mean(dzg * unit, axis=1, keepdims=True))
+            dy_s[...] = (dy_s[...].astype(F32) + dx).astype(BF16)
+
+        return carry
+
+    lax.fori_loop(0, layers, backward, 0)
+
+
+def reduce_kernel(
+    z_ref, g_ref, out_ref, zr_s, gr_s, part_s, r1_s, h_s, r2_s, k_s, r3_s,
+    core_send, core_recv, s1_send, s1_recv, s2_send, s2_recv, s3_send, s3_recv,
+):
+    me = lax.axis_index("dp")
+    core = lax.axis_index("pipe")
+    depth, share, hidden = out_ref.shape
+    nz = k_s.shape[1]
+    half = hidden // 2
+    x = me % 2
+    y = (me // 2) % 2
+    z = me // 4
+    x_mate = me + 1 - 2 * x
+    y_mate = me + 2 * (1 - 2 * y)
+    barrier = pltpu.get_barrier_semaphore()
+    mates = [(x_mate, core), (y_mate, core), (me, 1 - core)]
+    mates += [(((z + k) % nz) * 4 + me % 4, core) for k in range(1, nz)]
+    for mate in mates:
+        pl.semaphore_signal(barrier, inc=1, device_id=mate, device_id_type=MESH)
+    pl.semaphore_wait(barrier, len(mates))
+
+    def remote(src, dst, send, recv, mate):
+        return pltpu.make_async_remote_copy(
+            src_ref=src, dst_ref=dst, send_sem=send, recv_sem=recv,
+            device_id=mate, device_id_type=MESH,
+        )
+
+    sent = []
+    cores = []
+    for s in range(depth):
+        theirs = (1 - core) * depth + s
+        pair = []
+        for i, (src, dst) in enumerate(((z_ref, zr_s), (g_ref, gr_s))):
+            copy = remote(
+                src.at[theirs], dst.at[s], core_send.at[s, i], core_recv.at[s, i], (me, 1 - core)
+            )
+            copy.start()
+            pair.append(copy)
+        cores.append(pair)
+        sent += pair
+
+    pieces = [(s, c) for c in range(2) for s in range(depth)]
+    first = []
+    for p, (s, c) in enumerate(pieces):
+        if c == 0:
+            for copy in cores[s]:
+                copy.wait_recv()
+        cols = slice(c * half, (c + 1) * half)
+        mine = core * depth + s
+        part = dot(z_ref[mine], g_ref[mine, :, cols], 0, 0) + dot(zr_s[s], gr_s[s, :, cols], 0, 0)
+        part_s[p] = part.astype(BF16).reshape(nz, 2, 2, share, half)
+        if s % 2 == 0:
+            copy = remote(part_s.at[p, :, :, 1 - x], r1_s.at[p], s1_send.at[p], s1_recv.at[p], (x_mate, core))
+        else:
+            copy = remote(part_s.at[p, :, 1 - y], r1_s.at[p], s1_send.at[p], s1_recv.at[p], (y_mate, core))
+        copy.start()
+        first.append(copy)
+    second = []
+    for p, (s, c) in enumerate(pieces):
+        first[p].wait_recv()
+        if s % 2 == 0:
+            there, mate = 1 - y, (y_mate, core)
+            own = part_s[p, :, there, x]
+        else:
+            there, mate = 1 - x, (x_mate, core)
+            own = part_s[p, :, y, there]
+        h_s[p] = (own.astype(F32) + r1_s[p, :, there].astype(F32)).astype(BF16)
+        copy = remote(h_s.at[p], r2_s.at[p], s2_send.at[p], s2_recv.at[p], mate)
+        copy.start()
+        second.append(copy)
+    third = []
+    for p, (s, c) in enumerate(pieces):
+        second[p].wait_recv()
+        here = y if s % 2 == 0 else x
+        total = part_s[p, :, y, x].astype(F32) + r1_s[p, :, here].astype(F32)
+        k_s[p] = (total + r2_s[p].astype(F32)).astype(BF16)
+        row = []
+        for k in range(1, nz):
+            there = (z + k) % nz
+            copy = remote(
+                k_s.at[p, there], r3_s.at[p, k - 1], s3_send.at[p, k - 1], s3_recv.at[p, k - 1],
+                (there * 4 + me % 4, core),
+            )
+            copy.start()
+            row.append(copy)
+        third.append(row)
+    for p, (s, c) in enumerate(pieces):
+        total = k_s[p, z].astype(F32)
+        for k in range(1, nz):
+            third[p][k - 1].wait_recv()
+            total = total + r3_s[p, k - 1].astype(F32)
+        out_ref[s, :, c * half : (c + 1) * half] = total
+    for copy in sent + first + second + [copy for row in third for copy in row]:
+        copy.wait_send()
+
+
+def split_batches(blocks, dest, resets, w_query, gain, decay, cot):
+    groups = lax.axis_size("dp")
+    segments = lax.axis_size("pipe")
+    _, rows, width = blocks.shape
+    depth, _, hidden = w_query.shape
+    heads = decay.shape[1]
+    layers = depth * segments
+    room = (rows // CH + groups - 1) // groups
+    slot = (room * CH + 15) // 16 * 16
+    vmem = pl.BlockSpec(memory_space=pltpu.VMEM)
+    hbm = pl.BlockSpec(memory_space=pl.ANY)
+    dma = pltpu.SemaphoreType.DMA
+    limit = 50 * 2**20
+    received, w_all, gain_all, decay_all = pl.pallas_call(
+        functools.partial(exchange_kernel, groups, slot),
+        out_shape=(
+            jax.ShapeDtypeStruct((groups, slot, width), BF16),
+            jax.ShapeDtypeStruct((segments,) + w_query.shape, BF16),
+            jax.ShapeDtypeStruct((segments,) + gain.shape, F32),
+            jax.ShapeDtypeStruct((segments,) + decay.shape, F32),
+        ),
+        in_specs=[vmem, vmem, hbm, vmem, vmem],
+        out_specs=(vmem, hbm, vmem, vmem),
+        scratch_shapes=[
+            pltpu.VMEM((groups, slot, width), BF16),
+            dma((groups,)), dma((groups,)), dma((3,)), dma((3,)), dma((3,)),
+        ],
+        compiler_params=pltpu.CompilerParams(
+            collective_id=0, has_side_effects=True, vmem_limit_bytes=limit
+        ),
+        name="exchange",
+    )(blocks, dest, w_query, gain, decay)
+    z_all, g_all = pl.pallas_call(
+        functools.partial(layers_kernel, heads, slot),
+        out_shape=(
+            jax.ShapeDtypeStruct((layers, rows, width), BF16),
+            jax.ShapeDtypeStruct((layers, rows, hidden), BF16),
+        ),
+        in_specs=[vmem] * 7,
+        out_specs=(vmem, vmem),
+        scratch_shapes=[
+            pltpu.VMEM((layers, rows, hidden), BF16),
+            pltpu.VMEM((layers + 1, rows, width), BF16),
+            pltpu.VMEM((layers, heads, rows, rows), BF16),
+            pltpu.VMEM((layers, heads, rows, rows), F32),
+            pltpu.VMEM((layers, rows, width), F32),
+            pltpu.VMEM((layers, heads, rows, 1), F32),
+            pltpu.VMEM((layers, rows, 1), F32),
+            pltpu.VMEM((rows, width), BF16),
+            pltpu.VMEM((rows, width), F32),
+        ],
+        compiler_params=pltpu.CompilerParams(vmem_limit_bytes=limit),
+        name="layers",
+    )(received, dest, resets, w_all, gain_all, decay_all, cot)
+    share = width // groups
+    nz = groups // 4
+    pieces = 2 * depth
+    half = hidden // 2
+    return pl.pallas_call(
+        reduce_kernel,
+        out_shape=jax.ShapeDtypeStruct((depth, share, hidden), F32),
+        in_specs=[vmem, vmem],
+        out_specs=vmem,
+        scratch_shapes=[
+            pltpu.VMEM((depth, rows, width), BF16),
+            pltpu.VMEM((depth, rows, hidden), BF16),
+            pltpu.VMEM((pieces, nz, 2, 2, share, half), BF16),
+            pltpu.VMEM((pieces, nz, 2, share, half), BF16),
+            pltpu.VMEM((pieces, nz, share, half), BF16),
+            pltpu.VMEM((pieces, nz, share, half), BF16),
+            pltpu.VMEM((pieces, nz, share, half), BF16),
+            pltpu.VMEM((pieces, nz - 1, share, half), BF16),
+            dma((depth, 2)), dma((depth, 2)),
+            dma((pieces,)), dma((pieces,)), dma((pieces,)), dma((pieces,)),
+            dma((pieces, nz - 1)), dma((pieces, nz - 1)),
+        ],
+        compiler_params=pltpu.CompilerParams(
+            collective_id=1, has_side_effects=True, vmem_limit_bytes=limit
+        ),
+        name="reduce",
+    )(z_all, g_all)
+
+
+def local(blocks, dest, resets, w_query, gain, decay, cot):
+    groups = lax.axis_size("dp")
+    segments = lax.axis_size("pipe")
+    if segments == 2 and blocks.shape[0] == segments and groups == 16:
+        return split_batches(blocks, dest, resets, w_query, gain, decay, cot)
+    return pipelined(blocks, dest, resets, w_query, gain, decay, cot)
+
+
 def solution(mesh):
     placed = (
         P(None, "dp", None),

time: 481 us -> 77.7 us (0.16)
  waiting for transfers between devices: 214 us -> 0 us
  other arithmetic: 72.5 us -> 0 us
  Pallas kernels: 0 us -> 71.8 us
  matrix products: 63.1 us -> 0 us
  starting transfers between devices: 60.2 us -> 0 us
  local copies, waits for them, and re-layouts: 52.6 us -> 5.53 us
  between operations: 13.5 us -> 0.05 us
    psum x1 -> x0, waiting for transfers between devices: 167 us -> none  [local(): full = lax.psum(grad_total, 'dp')]
    pallas_call x0 -> x3, Pallas kernels: none -> 71.8 us  [the longest x1 38.2 us: split_batches(): pl.pallas_call(reduce_kernel, out_shape=jax.ShapeDtypeStruct((depth, shar...]
    dot_general x44 -> x0, matrix products: 63.1 us -> none  [the longest x12 24.1 us: normed_project(): jnp.dot(z, weight, preferred_element_type=jnp.float32) + extra]
    ppermute x6 -> x0, starting transfers between devices: 52.8 us -> none  [shifted(): return lax.ppermute(x, axis, pairs)]
    ppermute x6 -> x0, waiting for transfers between devices: 31.4 us -> none  [shifted(): return lax.ppermute(x, axis, pairs)]
    add x4 -> x0, other arithmetic: 18 us -> none  [the longest x3 18 us: backward_tick(): return (inbox, grad_total + d_weight)]
    all_to_all x1 -> x0, waiting for transfers between devices: 15.4 us -> none  [local(): lax.all_to_all(outgoing, 'dp', split_axis=1, concat_axis=1, tiled=True)]
    convert_element_type x13 -> x0, local copies, waits for them, and re-layouts: 15 us -> none  [the longest x12 13.3 us: normed_project(): (jnp.dot(z, weight, preferred_element_type=jnp.float32) + extra).astype(j...]
  transfers between devices with their start and end apart: 8 -> 0, of which waited for: 5 -> 0; matrix products, arithmetic and copies ran while one was open for 4% -> 0% of each run, Pallas kernels for 0% -> 0%
where the time goes in v1:
time: 77.7 us; the launch traced here: 77.3 us
  Pallas kernels  71.8 us (92%)
  local copies, waits for them, and re-layouts  5.53 us (7%)
    pallas_call x1, Pallas kernels, split_batches(): pl.pallas_call(reduce_kernel, out_shape=jax.ShapeDtypeStruct((depth, shar...  38.2 us
    pallas_call x1, Pallas kernels, split_batches(): pl.pallas_call(functools.partial(layers_kernel, heads, slot), out_shape=(...  19.3 us
    pallas_call x1, Pallas kernels, split_batches(): pl.pallas_call(functools.partial(exchange_kernel, groups, slot), out_shap...  14.2 us
    unnamed x15, local copies, waits for them, and re-layouts  5.53 us

profile of v1, /device:TPU:1, one launch (start us, length us, event | category | flops | bytes accessed | tf_op | source)
XLA Modules:
  0.0 77.3 jit_solution(1227150737047354991)
XLA Ops:
  0.0 0.0 copy-start
  0.0 1.6 %copy-done = bf16[2,1024,512]{2,1,0:T(8,128)(2,1)S(1)} copy-done((bf16[2,1024,512]{2,1,0:T(8,128)(2,1)S(1)}, bf16[2,1024,512]{2,1,0:T(8,128)(2,1)}, u32[]{:S(2)}) %copy-start) | copy-done | bytes 2097176
  1.6 0.0 copy-start.1
  1.6 1.1 %copy-done.1 = bf16[2,192,1024]{2,1,0:T(8,128)(2,1)S(1)} copy-done((bf16[2,192,1024]{2,1,0:T(8,128)(2,1)S(1)}, bf16[2,192,1024]{2,1,0:T(8,128)(2,1)}, u32[]{:S(2)}) %copy-start.1) | copy-done | bytes 786456
  2.7 0.0 copy-start.3
  2.7 0.7 copy-done.3
  3.4 0.0 copy-start.4
  3.4 0.7 copy-done.4
  4.1 0.0 copy-start.5
  4.1 0.7 copy-done.5
  4.8 0.0 copy-start.2
  4.8 0.0 copy-start.6
  4.8 14.2 %exchange.1 = (bf16[16,16,1024]{2,1,0:T(8,128)(2,1)S(1)}, bf16[2,2,1024,512]{3,2,1,0:T(8,128)(2,1)}, f32[2,2,1024]{2,1,0:T(2,128)S(1)}, f32[2,2,8]{2,1,0:T(2,128)S(1)}) custom-call(bf16[2,192,1024]{2,1,0:T(8,128)(2,1)S(1)} %copy-done.1, s32[2,16,48]{2,1,0:T(8,128)S(1)} %copy-done.3, bf16[2,1024,512]{2,1,0:T(8,128)(2,1)S(1)} %copy-done, ...), custom_call_target="tpu_custom_call" | custom-call | tf_op jit(solution)/shard_map/exchange/pallas_call | solution.py:491
  19.1 0.0 copy-done.2
  19.1 0.0 copy-done.6
  19.1 19.3 %layers.1 = (bf16[4,192,1024]{2,1,0:T(8,128)(2,1)S(1)}, bf16[4,192,512]{2,1,0:T(8,128)(2,1)S(1)}) custom-call(bf16[16,16,1024]{2,1,0:T(8,128)(2,1)S(1)} %get-tuple-element.11.recv_ref, s32[2,16,48]{2,1,0:T(8,128)S(1)} %copy-done.3, s32[2,32]{1,0:T(2,128)S(1)} %copy-done.6, bf16[2,2,1024,512]{3,2,1,0:T(8,128)(2,1)} %get-tuple-element.12.w_ref, ...), custom_call_target="tpu_custom_call" | custom-call | tf_op jit(solution)/shard_map/layers/pallas_call | solution.py:510
  38.4 38.2 %reduce.1 = f32[2,64,512]{2,1,0:T(8,128)S(1)} custom-call(bf16[4,192,1024]{2,1,0:T(8,128)(2,1)S(1)} %get-tuple-element.15.z_ref, bf16[4,192,512]{2,1,0:T(8,128)(2,1)S(1)} %get-tuple-element.16.g_ref), custom_call_target="tpu_custom_call" | custom-call | tf_op jit(solution)/shard_map/reduce/pallas_call | solution.py:536
  76.6 0.7 copy.9
Async XLA Ops:
  0.0 1.6 %copy-start = (bf16[2,1024,512]{2,1,0:T(8,128)(2,1)S(1)}, bf16[2,1024,512]{2,1,0:T(8,128)(2,1)}, u32[]{:S(2)}) copy-start(bf16[2,1024,512]{2,1,0:T(8,128)(2,1)} %w_ref.1) | copy-start | bytes 6291460
  1.6 1.1 %copy-start.1 = (bf16[2,192,1024]{2,1,0:T(8,128)(2,1)S(1)}, bf16[2,192,1024]{2,1,0:T(8,128)(2,1)}, u32[]{:S(2)}) copy-start(bf16[2,192,1024]{2,1,0:T(8,128)(2,1)} %blocks_ref.1) | copy-start | bytes 2359300
  2.7 0.7 copy-start.3
  3.4 0.7 copy-start.4
  4.1 0.7 copy-start.5
  4.8 14.3 %copy-start.2 = (bf16[2,192,1024]{2,1,0:T(8,128)(2,1)S(1)}, bf16[2,192,1024]{2,1,0:T(8,128)(2,1)}, u32[]{:S(2)}) copy-start(bf16[2,192,1024]{2,1,0:T(8,128)(2,1)} %cot_ref.1) | copy-start | bytes 2359300
  4.8 14.3 %copy-start.6 = (s32[2,32]{1,0:T(2,128)S(1)}, s32[2,32]{1,0:T(2,128)}, u32[]{:S(2)}) copy-start(s32[2,32]{1,0:T(2,128)} %resets_ref.1) | copy-start | bytes 772

commit v2 on v1

--- a/solution.py
+++ b/solution.py
@@ -208,11 +208,18 @@
 
 def exchange_kernel(
     groups, slot, blocks_ref, dest_ref, w_ref, gain_ref, decay_ref,
-    recv_ref, w_all, gain_all, decay_all, out_s, send_sem, recv_sem, par_send, par_recv, own_sem,
+    recv_ref, w_all, gain_all, decay_all,
+    in_s, dest_s, out_s, in_sem, send_sem, recv_sem, par_send, par_recv, own_sem,
 ):
     me = lax.axis_index("dp")
     core = lax.axis_index("pipe")
     barrier = pltpu.get_barrier_semaphore()
+    loads = [
+        pltpu.make_async_copy(dest_ref.at[core], dest_s, in_sem.at[0]),
+        pltpu.make_async_copy(blocks_ref.at[core], in_s, in_sem.at[1]),
+    ]
+    for load in loads:
+        load.start()
 
     def greet(k, carry):
         pl.semaphore_signal(
@@ -232,7 +239,8 @@
     rows = blocks_ref.shape[1]
     per_rank = rows // CH
     total = groups * slot
-    own_row = dest_ref[core, pl.ds(me, 1), :]
+    loads[0].wait()
+    own_row = dest_s[pl.ds(me, 1), :]
     own_col = as_column(own_row)
     order = (per_rank, per_rank)
     earlier = (own_row == own_col) & (iota(order, 1) < iota(order, 0))
@@ -243,7 +251,8 @@
     target_row = jnp.sum(jnp.where(spread, jnp.broadcast_to(target, wide), 0), axis=0, keepdims=True)
     target_row = target_row + iota((1, rows), 1) % CH
     send_map = jnp.where(iota((total, rows), 0) == target_row, 1.0, 0.0).astype(BF16)
-    picked = dot(send_map, blocks_ref[core]).astype(BF16)
+    loads[1].wait()
+    picked = dot(send_map, in_s[...]).astype(BF16)
     out_s[...] = picked.reshape(out_s.shape)
 
     pl.semaphore_wait(barrier, groups)
@@ -283,19 +292,52 @@
 
 
 def layers_kernel(
-    heads, slot, recv_ref, dest_ref, resets_ref, w_ref, gain_ref, decay_ref, cot_ref,
-    z_ref, g_ref, q_s, x_s, a_s, table_s, n_s, ro_s, r_s, dy_s, dv_s,
+    heads, slot, recv_ref, dest_ref, resets_ref, w_ref, gain_ref, decay_ref, cot_ref, out_ref,
+    dest_s, resets_s, z_s, g_s, q_s, x_s, a_s, table_s, n_s, ro_s, r_s, dy_s, dv_s,
+    zr_s, gr_s, part_s, r1_s, h_s, r2_s, k_s, r3_s, fin_s, finr_s,
+    in_sem, z_send, z_recv, g_send, g_recv, s1_send, s1_recv, s2_send, s2_recv,
+    s3_send, s3_recv, f_send, f_recv,
 ):
     me = lax.axis_index("dp")
     core = lax.axis_index("pipe")
-    layers, rows, width = z_ref.shape
-    depth = w_ref.shape[1]
-    dk = g_ref.shape[2] // heads
+    layers, rows, width = z_s.shape
+    depth, share, hidden = out_ref.shape
+    half = hidden // 2
+    nz = k_s.shape[1]
+    dk = hidden // heads
     dv = width // heads
     per_rank = rows // CH
     groups = dest_ref.shape[1]
-
-    hits = jnp.where(dest_ref[core] == me, 1.0, 0.0)
+    x = me % 2
+    y = (me // 2) % 2
+    z_at = me // 4
+    x_mate = me + 1 - 2 * x
+    y_mate = me + 2 * (1 - 2 * y)
+    peer = (me, 1 - core)
+    loads = [
+        pltpu.make_async_copy(dest_ref.at[core], dest_s, in_sem.at[0]),
+        pltpu.make_async_copy(resets_ref, resets_s, in_sem.at[1]),
+        pltpu.make_async_copy(cot_ref.at[core], dy_s, in_sem.at[2]),
+    ]
+    for load in loads:
+        load.start()
+    barrier = pltpu.get_barrier_semaphore()
+    mates = [(x_mate, core), (y_mate, core), peer]
+    mates += [(((z_at + k) % nz) * 4 + me % 4, core) for k in range(1, nz)]
+    for mate in mates:
+        pl.semaphore_signal(barrier, inc=1, device_id=mate, device_id_type=MESH)
+
+    def remote(src, dst, send, recv, mate):
+        return pltpu.make_async_remote_copy(
+            src_ref=src, dst_ref=dst, send_sem=send, recv_sem=recv,
+            device_id=mate, device_id_type=MESH,
+        )
+
+    def z_copy(l):
+        return remote(z_s.at[l], zr_s.at[l], z_send.at[l], z_recv.at[l], peer)
+
+    loads[0].wait()
+    hits = jnp.where(dest_s[...] == me, 1.0, 0.0)
     order = (per_rank, per_rank)
     upper = jnp.where(iota(order, 0) < iota(order, 1), 1.0, 0.0).astype(BF16)
     before = dot(hits.astype(BF16), upper)
@@ -308,7 +350,8 @@
     recv_map = jnp.where(iota((rows, groups * slot), 1) == source_col, 1.0, 0.0).astype(BF16)
     x_s[0] = dot(recv_map, recv_ref[...].reshape(groups * slot, width)).astype(BF16)
 
-    resets = resets_ref[pl.ds(core, 1), :]
+    loads[1].wait()
+    resets = resets_s[pl.ds(core, 1), :]
     n_resets = resets.shape[1]
     start = me * rows
     count_col = jnp.sum(
@@ -322,13 +365,16 @@
     same = (count_col == count_row) & (steps >= 0)
     diff = steps.astype(F32)
 
+    pl.semaphore_wait(barrier, len(mates))
+
     def forward(l, carry):
         x32 = x_s[l].astype(F32)
         scale = lax.rsqrt(jnp.mean(x32 * x32, axis=1, keepdims=True) + EPS)
         r_s[l] = scale
         gain = gain_ref[l // depth, pl.ds(l % depth, 1), :]
         z = (x32 * scale * gain).astype(BF16)
-        z_ref[l] = z
+        z_s[l] = z
+        z_copy(l).start()
         q = dot(z, w_ref[l // depth, l % depth]).astype(BF16)
         q_s[l] = q
         rates = jnp.log(decay_ref[l // depth, pl.ds(l % depth, 1), :])
@@ -348,25 +394,75 @@
         return carry
 
     lax.fori_loop(0, layers, forward, 0)
-    dy_s[...] = cot_ref[core]
-
-    def backward(i, carry):
-        l = layers - 1 - i
+    loads[2].wait()
+    copies = {}
+
+    def begin(name, copy):
+        copy.start()
+        copies[name] = copy
+
+    def places(l):
+        by_x = (core + l) % 2
+        by_y = 1 - by_x
+        first = (by_x * x_mate + by_y * y_mate, core)
+        second = (by_x * y_mate + by_y * x_mate, core)
+        return by_x, by_y, by_x * x + by_y * y, by_x * y + by_y * x, first, second
+
+    def weight_part(l):
+        by_x, by_y, f, s, first, second = places(l)
+        copies["g", l].wait_recv()
+        z_copy(l).wait_recv()
+        part = dot(z_s[l], g_s[l, core], 0, 0) + dot(zr_s[l], gr_s[l], 0, 0)
+        for d in range(groups):
+            zd, yd, xd = d // 4, (d // 2) % 2, d % 2
+            rows_d = part[d * share : (d + 1) * share].astype(BF16)
+            part_s[l, by_x * xd + by_y * yd, by_x * yd + by_y * xd, zd] = rows_d
+        begin(("s1", l), remote(part_s.at[l, 1 - f], r1_s.at[l], s1_send.at[l], s1_recv.at[l], first))
+
+    def stage_two(l):
+        _, _, f, s, first, second = places(l)
+        copies["s1", l].wait_recv()
+        total = part_s[l, f, 1 - s].astype(F32) + r1_s[l, 1 - s].astype(F32)
+        h_s[l] = total.astype(BF16)
+        begin(("s2", l), remote(h_s.at[l], r2_s.at[l], s2_send.at[l], s2_recv.at[l], second))
+
+    def stage_three(l):
+        _, _, f, s, first, second = places(l)
+        copies["s2", l].wait_recv()
+        total = part_s[l, f, s].astype(F32) + r1_s[l, s].astype(F32) + r2_s[l].astype(F32)
+        k_s[l] = total.astype(BF16)
+        for k in range(1, nz):
+            there = (z_at + k) % nz
+            begin(("s3", l, k), remote(
+                k_s.at[l, there], r3_s.at[l, k - 1], s3_send.at[l, k - 1], s3_recv.at[l, k - 1],
+                (there * 4 + me % 4, core),
+            ))
+
+    def finish_sum(l):
+        total = k_s[l, z_at].astype(F32)
+        for k in range(1, nz):
+            copies["s3", l, k].wait_recv()
+            total = total + r3_s[l, k - 1].astype(F32)
+        fin_s[l] = total
+
+    def backward(l):
         for h in range(heads):
             cols = slice(h * dv, (h + 1) * dv)
             dn = dy_s[:, cols].astype(F32)
             n = n_s[l, :, cols]
             do = ro_s[l, h] * (dn - n * jnp.mean(dn * n, axis=1, keepdims=True))
             do = do.astype(BF16)
-            da = dot(do, z_ref[l, :, cols], 1, 1)
+            da = dot(do, z_s[l, :, cols], 1, 1)
             ds = (da * table_s[l, h]).astype(BF16)
-            dv_s[:, cols] = dot(a_s[l, h], do, 0, 0)
+            if l > 0:
+                dv_s[:, cols] = dot(a_s[l, h], do, 0, 0)
             qh = q_s[l, :, h * dk : (h + 1) * dk]
-            g_ref[l, :, h * dk : (h + 1) * dk] = (dot(ds, qh) + dot(ds, qh, 0, 0)).astype(BF16)
-
-        @pl.when(l > 0)
-        def _():
-            dz = dot(g_ref[l], w_ref[l // depth, l % depth], 1, 1) + dv_s[...]
+            at = h * dk % half
+            g_s[l, h * dk // half, :, at : at + dk] = (dot(ds, qh) + dot(ds, qh, 0, 0)).astype(BF16)
+        begin(("g", l), remote(g_s.at[l, 1 - core], gr_s.at[l], g_send.at[l], g_recv.at[l], peer))
+        if l > 0:
+            w = w_ref[l // depth, l % depth]
+            dz = dot(g_s[l, 0], w[:, :half], 1, 1) + dot(g_s[l, 1], w[:, half:], 1, 1) + dv_s[...]
             gain = gain_ref[l // depth, pl.ds(l % depth, 1), :]
             scale = r_s[l]
             unit = x_s[l].astype(F32) * scale
@@ -374,105 +470,32 @@
             dx = scale * (dzg - unit * jnp.mean(dzg * unit, axis=1, keepdims=True))
             dy_s[...] = (dy_s[...].astype(F32) + dx).astype(BF16)
 
-        return carry
-
-    lax.fori_loop(0, layers, backward, 0)
-
-
-def reduce_kernel(
-    z_ref, g_ref, out_ref, zr_s, gr_s, part_s, r1_s, h_s, r2_s, k_s, r3_s,
-    core_send, core_recv, s1_send, s1_recv, s2_send, s2_recv, s3_send, s3_recv,
-):
-    me = lax.axis_index("dp")
-    core = lax.axis_index("pipe")
-    depth, share, hidden = out_ref.shape
-    nz = k_s.shape[1]
-    half = hidden // 2
-    x = me % 2
-    y = (me // 2) % 2
-    z = me // 4
-    x_mate = me + 1 - 2 * x
-    y_mate = me + 2 * (1 - 2 * y)
-    barrier = pltpu.get_barrier_semaphore()
-    mates = [(x_mate, core), (y_mate, core), (me, 1 - core)]
-    mates += [(((z + k) % nz) * 4 + me % 4, core) for k in range(1, nz)]
-    for mate in mates:
-        pl.semaphore_signal(barrier, inc=1, device_id=mate, device_id_type=MESH)
-    pl.semaphore_wait(barrier, len(mates))
-
-    def remote(src, dst, send, recv, mate):
-        return pltpu.make_async_remote_copy(
-            src_ref=src, dst_ref=dst, send_sem=send, recv_sem=recv,
-            device_id=mate, device_id_type=MESH,
-        )
-
-    sent = []
-    cores = []
+    for step in range(layers + 3):
+        l = layers - 1 - step
+        if l >= 0:
+            backward(l)
+            weight_part(l)
+        if 0 <= l + 1 < layers:
+            stage_two(l + 1)
+        if 0 <= l + 2 < layers:
+            stage_three(l + 2)
+        if 0 <= l + 3 < layers:
+            finish_sum(l + 3)
+
     for s in range(depth):
         theirs = (1 - core) * depth + s
-        pair = []
-        for i, (src, dst) in enumerate(((z_ref, zr_s), (g_ref, gr_s))):
-            copy = remote(
-                src.at[theirs], dst.at[s], core_send.at[s, i], core_recv.at[s, i], (me, 1 - core)
-            )
-            copy.start()
-            pair.append(copy)
-        cores.append(pair)
-        sent += pair
-
-    pieces = [(s, c) for c in range(2) for s in range(depth)]
-    first = []
-    for p, (s, c) in enumerate(pieces):
-        if c == 0:
-            for copy in cores[s]:
-                copy.wait_recv()
-        cols = slice(c * half, (c + 1) * half)
-        mine = core * depth + s
-        part = dot(z_ref[mine], g_ref[mine, :, cols], 0, 0) + dot(zr_s[s], gr_s[s, :, cols], 0, 0)
-        part_s[p] = part.astype(BF16).reshape(nz, 2, 2, share, half)
-        if s % 2 == 0:
-            copy = remote(part_s.at[p, :, :, 1 - x], r1_s.at[p], s1_send.at[p], s1_recv.at[p], (x_mate, core))
-        else:
-            copy = remote(part_s.at[p, :, 1 - y], r1_s.at[p], s1_send.at[p], s1_recv.at[p], (y_mate, core))
-        copy.start()
-        first.append(copy)
-    second = []
-    for p, (s, c) in enumerate(pieces):
-        first[p].wait_recv()
-        if s % 2 == 0:
-            there, mate = 1 - y, (y_mate, core)
-            own = part_s[p, :, there, x]
-        else:
-            there, mate = 1 - x, (x_mate, core)
-            own = part_s[p, :, y, there]
-        h_s[p] = (own.astype(F32) + r1_s[p, :, there].astype(F32)).astype(BF16)
-        copy = remote(h_s.at[p], r2_s.at[p], s2_send.at[p], s2_recv.at[p], mate)
-        copy.start()
-        second.append(copy)
-    third = []
-    for p, (s, c) in enumerate(pieces):
-        second[p].wait_recv()
-        here = y if s % 2 == 0 else x
-        total = part_s[p, :, y, x].astype(F32) + r1_s[p, :, here].astype(F32)
-        k_s[p] = (total + r2_s[p].astype(F32)).astype(BF16)
-        row = []
-        for k in range(1, nz):
-            there = (z + k) % nz
-            copy = remote(
-                k_s.at[p, there], r3_s.at[p, k - 1], s3_send.at[p, k - 1], s3_recv.at[p, k - 1],
-                (there * 4 + me % 4, core),
-            )
-            copy.start()
-            row.append(copy)
-        third.append(row)
-    for p, (s, c) in enumerate(pieces):
-        total = k_s[p, z].astype(F32)
-        for k in range(1, nz):
-            third[p][k - 1].wait_recv()
-            total = total + r3_s[p, k - 1].astype(F32)
-        out_ref[s, :, c * half : (c + 1) * half] = total
-    for copy in sent + first + second + [copy for row in third for copy in row]:
+        begin(("f", s), remote(fin_s.at[theirs], finr_s.at[s], f_send.at[s], f_recv.at[s], peer))
+    mine = pl.ds(pl.multiple_of(core * half, half), half)
+    other = pl.ds(pl.multiple_of((1 - core) * half, half), half)
+    for s in range(depth):
+        out_ref[s, :, mine] = fin_s[core * depth + s]
+    for s in range(depth):
+        copies["f", s].wait_recv()
+        out_ref[s, :, other] = finr_s[s]
+    for copy in copies.values():
         copy.wait_send()
+    for l in range(layers):
+        z_copy(l).wait_send()
 
 
 def split_batches(blocks, dest, resets, w_query, gain, decay, cot):
@@ -485,9 +508,9 @@
     room = (rows // CH + groups - 1) // groups
     slot = (room * CH + 15) // 16 * 16
     vmem = pl.BlockSpec(memory_space=pltpu.VMEM)
-    hbm = pl.BlockSpec(memory_space=pl.ANY)
+    hbm = pl.BlockSpec(memory_space=pltpu.HBM)
     dma = pltpu.SemaphoreType.DMA
-    limit = 50 * 2**20
+    limit = 63 * 2**20
     received, w_all, gain_all, decay_all = pl.pallas_call(
         functools.partial(exchange_kernel, groups, slot),
         out_shape=(
@@ -496,26 +519,32 @@
             jax.ShapeDtypeStruct((segments,) + gain.shape, F32),
             jax.ShapeDtypeStruct((segments,) + decay.shape, F32),
         ),
-        in_specs=[vmem, vmem, hbm, vmem, vmem],
-        out_specs=(vmem, hbm, vmem, vmem),
+        in_specs=[hbm] * 5,
+        out_specs=(vmem, vmem, vmem, vmem),
         scratch_shapes=[
+            pltpu.VMEM((rows, width), BF16),
+            pltpu.VMEM(dest.shape[1:], jnp.int32),
             pltpu.VMEM((groups, slot, width), BF16),
-            dma((groups,)), dma((groups,)), dma((3,)), dma((3,)), dma((3,)),
+            dma((2,)), dma((groups,)), dma((groups,)), dma((3,)), dma((3,)), dma((3,)),
         ],
         compiler_params=pltpu.CompilerParams(
             collective_id=0, has_side_effects=True, vmem_limit_bytes=limit
         ),
         name="exchange",
     )(blocks, dest, w_query, gain, decay)
-    z_all, g_all = pl.pallas_call(
+    share = width // groups
+    nz = groups // 4
+    half = hidden // 2
+    return pl.pallas_call(
         functools.partial(layers_kernel, heads, slot),
-        out_shape=(
-            jax.ShapeDtypeStruct((layers, rows, width), BF16),
-            jax.ShapeDtypeStruct((layers, rows, hidden), BF16),
-        ),
-        in_specs=[vmem] * 7,
-        out_specs=(vmem, vmem),
+        out_shape=jax.ShapeDtypeStruct((depth, share, hidden), F32),
+        in_specs=[vmem, hbm, hbm, vmem, vmem, vmem, hbm],
+        out_specs=vmem,
         scratch_shapes=[
+            pltpu.VMEM(dest.shape[1:], jnp.int32),
+            pltpu.VMEM(resets.shape, jnp.int32),
+            pltpu.VMEM((layers, rows, width), BF16),
+            pltpu.VMEM((layers, 2, rows, half), BF16),
             pltpu.VMEM((layers, rows, hidden), BF16),
             pltpu.VMEM((layers + 1, rows, width), BF16),
             pltpu.VMEM((layers, heads, rows, rows), BF16),
@@ -525,37 +554,25 @@
             pltpu.VMEM((layers, rows, 1), F32),
             pltpu.VMEM((rows, width), BF16),
             pltpu.VMEM((rows, width), F32),
-        ],
-        compiler_params=pltpu.CompilerParams(vmem_limit_bytes=limit),
-        name="layers",
-    )(received, dest, resets, w_all, gain_all, decay_all, cot)
-    share = width // groups
-    nz = groups // 4
-    pieces = 2 * depth
-    half = hidden // 2
-    return pl.pallas_call(
-        reduce_kernel,
-        out_shape=jax.ShapeDtypeStruct((depth, share, hidden), F32),
-        in_specs=[vmem, vmem],
-        out_specs=vmem,
-        scratch_shapes=[
-            pltpu.VMEM((depth, rows, width), BF16),
-            pltpu.VMEM((depth, rows, hidden), BF16),
-            pltpu.VMEM((pieces, nz, 2, 2, share, half), BF16),
-            pltpu.VMEM((pieces, nz, 2, share, half), BF16),
-            pltpu.VMEM((pieces, nz, share, half), BF16),
-            pltpu.VMEM((pieces, nz, share, half), BF16),
-            pltpu.VMEM((pieces, nz, share, half), BF16),
-            pltpu.VMEM((pieces, nz - 1, share, half), BF16),
-            dma((depth, 2)), dma((depth, 2)),
-            dma((pieces,)), dma((pieces,)), dma((pieces,)), dma((pieces,)),
-            dma((pieces, nz - 1)), dma((pieces, nz - 1)),
+            pltpu.VMEM((layers, rows, width), BF16),
+            pltpu.VMEM((layers, rows, half), BF16),
+            pltpu.VMEM((layers, 2, 2, nz, share, half), BF16),
+            pltpu.VMEM((layers, 2, nz, share, half), BF16),
+            pltpu.VMEM((layers, nz, share, half), BF16),
+            pltpu.VMEM((layers, nz, share, half), BF16),
+            pltpu.VMEM((layers, nz, share, half), BF16),
+            pltpu.VMEM((layers, nz - 1, share, half), BF16),
+            pltpu.VMEM((layers, share, half), F32),
+            pltpu.VMEM((depth, share, half), F32),
+            dma((3,)), dma((layers,)), dma((layers,)), dma((layers,)), dma((layers,)),
+            dma((layers,)), dma((layers,)), dma((layers,)), dma((layers,)),
+            dma((layers, nz - 1)), dma((layers, nz - 1)), dma((depth,)), dma((depth,)),
         ],
         compiler_params=pltpu.CompilerParams(
             collective_id=1, has_side_effects=True, vmem_limit_bytes=limit
         ),
-        name="reduce",
-    )(z_all, g_all)
+        name="layers",
+    )(received, dest, resets, w_all, gain_all, decay_all, cot)
 
 
 def local(blocks, dest, resets, w_query, gain, decay, cot):

time: 77.7 us -> 68.5 us (0.88)
  Pallas kernels: 71.8 us -> 66.5 us
  local copies, waits for them, and re-layouts: 5.53 us -> 1.67 us
    pallas_call x2 -> x1, Pallas kernels: 57.5 us -> 50.1 us  [split_batches(): pl.pallas_call(functools.partial(layers_kernel, heads, slot), out_shape=j...]
    unnamed x15 -> x1, local copies, waits for them, and re-layouts: 5.53 us -> 1.67 us
    pallas_call x1, Pallas kernels: 14.2 us -> 16.4 us  [split_batches(): pl.pallas_call(functools.partial(exchange_kernel, groups, slot), out_shap...]
where the time goes in v2:
time: 68.5 us; the launch traced here: 68.2 us
  Pallas kernels  66.5 us (97%)
  local copies, waits for them, and re-layouts  1.67 us (2%)
    pallas_call x1, Pallas kernels, split_batches(): pl.pallas_call(functools.partial(layers_kernel, heads, slot), out_shape=j...  50.1 us
    pallas_call x1, Pallas kernels, split_batches(): pl.pallas_call(functools.partial(exchange_kernel, groups, slot), out_shap...  16.4 us
    unnamed x1, local copies, waits for them, and re-layouts  1.67 us

profile of v2, /device:TPU:1, one launch (start us, length us, event | category | flops | bytes accessed | tf_op | source)
XLA Modules:
  0.0 68.2 jit_solution(10931882613292600041)
XLA Ops:
  0.0 16.4 %exchange.1 = (bf16[16,16,1024]{2,1,0:T(8,128)(2,1)}, bf16[2,2,1024,512]{3,2,1,0:T(8,128)(2,1)}, f32[2,2,1024]{2,1,0:T(2,128)}, f32[2,2,8]{2,1,0:T(2,128)}) custom-call(bf16[2,192,1024]{2,1,0:T(8,128)(2,1)} %blocks_ref.1, s32[2,16,48]{2,1,0:T(8,128)} %dest_ref.3, bf16[2,1024,512]{2,1,0:T(8,128)(2,1)} %w_ref.1, f32[2,1024]{1,0:T(2,128)} %gain_ref.1, ...), custom_call_target="tpu_custom_call" | custom-call | tf_op jit(solution)/shard_map/exchange/pallas_call | solution.py:514
  16.4 50.1 %layers.1 = f32[2,64,512]{2,1,0:T(8,128)} custom-call(bf16[16,16,1024]{2,1,0:T(8,128)(2,1)} %get-tuple-element.9.recv_ref, s32[2,16,48]{2,1,0:T(8,128)} %dest_ref.3, s32[2,32]{1,0:T(2,128)} %resets_ref.1, bf16[2,2,1024,512]{3,2,1,0:T(8,128)(2,1)} %get-tuple-element.10.w_ref, f32[2,2,1024]{2,1,0:T(2,128)} %get-tuple-element.11.gain_ref, ...), custom_call_target="tpu_custom_call" | custom-call | tf_op jit(solution)/shard_map/layers/pallas_call | solution.py:538
  66.5 1.7 %copy.9 = f32[2,64,512]{2,1,0:T(8,128)} copy(f32[2,64,512]{2,1,0:T(8,128)} %layers.1) | data formatting | bytes 524288

commit v3 on v2

--- a/solution.py
+++ b/solution.py
@@ -206,7 +206,10 @@
     return jnp.sum(jnp.where(eye, jnp.broadcast_to(row, (n, n)), 0), axis=1, keepdims=True)
 
 
-def exchange_kernel(
+SPLIT = 4
+
+
+def begin_exchange(
     groups, slot, blocks_ref, dest_ref, w_ref, gain_ref, decay_ref,
     recv_ref, w_all, gain_all, decay_all,
     in_s, dest_s, out_s, in_sem, send_sem, recv_sem, par_send, par_recv, own_sem,
@@ -250,10 +253,14 @@
     spread = iota(wide, 1) // CH == iota(wide, 0)
     target_row = jnp.sum(jnp.where(spread, jnp.broadcast_to(target, wide), 0), axis=0, keepdims=True)
     target_row = target_row + iota((1, rows), 1) % CH
-    send_map = jnp.where(iota((total, rows), 0) == target_row, 1.0, 0.0).astype(BF16)
     loads[1].wait()
-    picked = dot(send_map, in_s[...]).astype(BF16)
-    out_s[...] = picked.reshape(out_s.shape)
+    lanes = in_s.shape[1] // SPLIT
+    picked = jnp.zeros((total, lanes), F32)
+    for c in range(SPLIT):
+        wanted = target_row + c * (slot // SPLIT)
+        send_map = jnp.where(iota((total, rows), 0) == wanted, 1.0, 0.0).astype(BF16)
+        picked = picked + dot(send_map, in_s[:, c * lanes : (c + 1) * lanes])
+    out_s[...] = picked.astype(BF16).reshape(out_s.shape)
 
     pl.semaphore_wait(barrier, groups)
 
@@ -279,20 +286,28 @@
         part.start()
         part_copies.append(part)
     recv_ref[me] = out_s[me]
-    for own in own_copies:
-        own.wait()
-
-    def arrive(k, carry):
-        pair_copy(k).wait()
-        return carry
-
-    lax.fori_loop(1, groups, arrive, 0)
-    for part in part_copies:
-        part.wait()
+
+    def scalars_here():
+        own_copies[2].wait()
+        part_copies[2].wait()
+
+    def rest_here():
+        for copy in own_copies[:2] + part_copies[:2]:
+            copy.wait()
+
+        def arrive(k, carry):
+            pair_copy(k).wait()
+            return carry
+
+        lax.fori_loop(1, groups, arrive, 0)
+
+    return scalars_here, rest_here
 
 
 def layers_kernel(
-    heads, slot, recv_ref, dest_ref, resets_ref, w_ref, gain_ref, decay_ref, cot_ref, out_ref,
+    heads, slot, blocks_ref, dest_ref, resets_ref, w_own, gain_own, decay_own, cot_ref, out_ref,
+    recv_ref, w_ref, gain_ref, decay_ref, blocks_s, out_s,
+    blocks_sem, send_sem, recv_sem, par_send, par_recv, own_sem,
     dest_s, resets_s, z_s, g_s, q_s, x_s, a_s, table_s, n_s, ro_s, r_s, dy_s, dv_s,
     zr_s, gr_s, part_s, r1_s, h_s, r2_s, k_s, r3_s, fin_s, finr_s,
     in_sem, z_send, z_recv, g_send, g_recv, s1_send, s1_recv, s2_send, s2_recv,
@@ -315,17 +330,16 @@
     y_mate = me + 2 * (1 - 2 * y)
     peer = (me, 1 - core)
     loads = [
-        pltpu.make_async_copy(dest_ref.at[core], dest_s, in_sem.at[0]),
-        pltpu.make_async_copy(resets_ref, resets_s, in_sem.at[1]),
-        pltpu.make_async_copy(cot_ref.at[core], dy_s, in_sem.at[2]),
+        pltpu.make_async_copy(resets_ref, resets_s, in_sem.at[0]),
+        pltpu.make_async_copy(cot_ref.at[core], dy_s, in_sem.at[1]),
     ]
     for load in loads:
         load.start()
-    barrier = pltpu.get_barrier_semaphore()
-    mates = [(x_mate, core), (y_mate, core), peer]
-    mates += [(((z_at + k) % nz) * 4 + me % 4, core) for k in range(1, nz)]
-    for mate in mates:
-        pl.semaphore_signal(barrier, inc=1, device_id=mate, device_id_type=MESH)
+    scalars_here, rest_here = begin_exchange(
+        groups, slot, blocks_ref, dest_ref, w_own, gain_own, decay_own,
+        recv_ref, w_ref, gain_ref, decay_ref, blocks_s, dest_s, out_s,
+        blocks_sem, send_sem, recv_sem, par_send, par_recv, own_sem,
+    )
 
     def remote(src, dst, send, recv, mate):
         return pltpu.make_async_remote_copy(
@@ -336,7 +350,6 @@
     def z_copy(l):
         return remote(z_s.at[l], zr_s.at[l], z_send.at[l], z_recv.at[l], peer)
 
-    loads[0].wait()
     hits = jnp.where(dest_s[...] == me, 1.0, 0.0)
     order = (per_rank, per_rank)
     upper = jnp.where(iota(order, 0) < iota(order, 1), 1.0, 0.0).astype(BF16)
@@ -347,10 +360,7 @@
     spread = iota(tall, 0) // CH == iota(tall, 1)
     source_col = jnp.sum(jnp.where(spread, jnp.broadcast_to(source, tall), 0.0), axis=1, keepdims=True)
     source_col = source_col.astype(jnp.int32) + iota((rows, 1), 0) % CH
-    recv_map = jnp.where(iota((rows, groups * slot), 1) == source_col, 1.0, 0.0).astype(BF16)
-    x_s[0] = dot(recv_map, recv_ref[...].reshape(groups * slot, width)).astype(BF16)
-
-    loads[1].wait()
+    loads[0].wait()
     resets = resets_s[pl.ds(core, 1), :]
     n_resets = resets.shape[1]
     start = me * rows
@@ -365,7 +375,22 @@
     same = (count_col == count_row) & (steps >= 0)
     diff = steps.astype(F32)
 
-    pl.semaphore_wait(barrier, len(mates))
+    scalars_here()
+
+    def fill(l, carry):
+        rates = jnp.log(decay_ref[l // depth, pl.ds(l % depth, 1), :])
+        for h in range(heads):
+            table_s[l, h] = jnp.where(same, jnp.exp(diff * rates[:, h : h + 1]), 0.0)
+        return carry
+
+    lax.fori_loop(0, layers, fill, 0)
+    rest_here()
+    lanes = width // SPLIT
+    arrived = recv_ref[...].reshape(groups * slot, lanes)
+    for c in range(SPLIT):
+        wanted = source_col + c * (slot // SPLIT)
+        recv_map = jnp.where(iota((rows, groups * slot), 1) == wanted, 1.0, 0.0).astype(BF16)
+        x_s[0, :, c * lanes : (c + 1) * lanes] = dot(recv_map, arrived).astype(BF16)
 
     def forward(l, carry):
         x32 = x_s[l].astype(F32)
@@ -377,10 +402,8 @@
         z_copy(l).start()
         q = dot(z, w_ref[l // depth, l % depth]).astype(BF16)
         q_s[l] = q
-        rates = jnp.log(decay_ref[l // depth, pl.ds(l % depth, 1), :])
         for h in range(heads):
-            table = jnp.where(same, jnp.exp(diff * rates[:, h : h + 1]), 0.0)
-            table_s[l, h] = table
+            table = table_s[l, h]
             qh = q[:, h * dk : (h + 1) * dk]
             a = (dot(qh, qh, 1, 1) * table).astype(BF16)
             a_s[l, h] = a
@@ -394,7 +417,7 @@
         return carry
 
     lax.fori_loop(0, layers, forward, 0)
-    loads[2].wait()
+    loads[1].wait()
     copies = {}
 
     def begin(name, copy):
@@ -410,9 +433,10 @@
 
     def weight_part(l):
         by_x, by_y, f, s, first, second = places(l)
+        part = dot(z_s[l], g_s[l, core], 0, 0)
         copies["g", l].wait_recv()
         z_copy(l).wait_recv()
-        part = dot(z_s[l], g_s[l, core], 0, 0) + dot(zr_s[l], gr_s[l], 0, 0)
+        part = part + dot(zr_s[l], gr_s[l], 0, 0)
         for d in range(groups):
             zd, yd, xd = d // 4, (d // 2) % 2, d % 2
             rows_d = part[d * share : (d + 1) * share].astype(BF16)
@@ -447,6 +471,8 @@
 
     def backward(l):
         for h in range(heads):
+            if h == heads // 2 and l + 1 < layers:
+                weight_part(l + 1)
             cols = slice(h * dv, (h + 1) * dv)
             dn = dy_s[:, cols].astype(F32)
             n = n_s[l, :, cols]
@@ -470,17 +496,18 @@
             dx = scale * (dzg - unit * jnp.mean(dzg * unit, axis=1, keepdims=True))
             dy_s[...] = (dy_s[...].astype(F32) + dx).astype(BF16)
 
-    for step in range(layers + 3):
+    for step in range(layers + 4):
         l = layers - 1 - step
         if l >= 0:
             backward(l)
-            weight_part(l)
-        if 0 <= l + 1 < layers:
-            stage_two(l + 1)
+        if l == -1:
+            weight_part(0)
         if 0 <= l + 2 < layers:
-            stage_three(l + 2)
+            stage_two(l + 2)
         if 0 <= l + 3 < layers:
-            finish_sum(l + 3)
+            stage_three(l + 3)
+        if 0 <= l + 4 < layers:
+            finish_sum(l + 4)
 
     for s in range(depth):
         theirs = (1 - core) * depth + s
@@ -506,41 +533,27 @@
     heads = decay.shape[1]
     layers = depth * segments
     room = (rows // CH + groups - 1) // groups
-    slot = (room * CH + 15) // 16 * 16
+    slot = room * CH * SPLIT
     vmem = pl.BlockSpec(memory_space=pltpu.VMEM)
     hbm = pl.BlockSpec(memory_space=pltpu.HBM)
     dma = pltpu.SemaphoreType.DMA
     limit = 63 * 2**20
-    received, w_all, gain_all, decay_all = pl.pallas_call(
-        functools.partial(exchange_kernel, groups, slot),
-        out_shape=(
-            jax.ShapeDtypeStruct((groups, slot, width), BF16),
-            jax.ShapeDtypeStruct((segments,) + w_query.shape, BF16),
-            jax.ShapeDtypeStruct((segments,) + gain.shape, F32),
-            jax.ShapeDtypeStruct((segments,) + decay.shape, F32),
-        ),
-        in_specs=[hbm] * 5,
-        out_specs=(vmem, vmem, vmem, vmem),
-        scratch_shapes=[
-            pltpu.VMEM((rows, width), BF16),
-            pltpu.VMEM(dest.shape[1:], jnp.int32),
-            pltpu.VMEM((groups, slot, width), BF16),
-            dma((2,)), dma((groups,)), dma((groups,)), dma((3,)), dma((3,)), dma((3,)),
-        ],
-        compiler_params=pltpu.CompilerParams(
-            collective_id=0, has_side_effects=True, vmem_limit_bytes=limit
-        ),
-        name="exchange",
-    )(blocks, dest, w_query, gain, decay)
     share = width // groups
     nz = groups // 4
     half = hidden // 2
     return pl.pallas_call(
         functools.partial(layers_kernel, heads, slot),
         out_shape=jax.ShapeDtypeStruct((depth, share, hidden), F32),
-        in_specs=[vmem, hbm, hbm, vmem, vmem, vmem, hbm],
+        in_specs=[hbm] * 7,
         out_specs=vmem,
         scratch_shapes=[
+            pltpu.VMEM((groups, slot, width // SPLIT), BF16),
+            pltpu.VMEM((segments,) + w_query.shape, BF16),
+            pltpu.VMEM((segments,) + gain.shape, F32),
+            pltpu.VMEM((segments,) + decay.shape, F32),
+            pltpu.VMEM((rows, width), BF16),
+            pltpu.VMEM((groups, slot, width // SPLIT), BF16),
+            dma((2,)), dma((groups,)), dma((groups,)), dma((3,)), dma((3,)), dma((3,)),
             pltpu.VMEM(dest.shape[1:], jnp.int32),
             pltpu.VMEM(resets.shape, jnp.int32),
             pltpu.VMEM((layers, rows, width), BF16),
@@ -564,15 +577,15 @@
             pltpu.VMEM((layers, nz - 1, share, half), BF16),
             pltpu.VMEM((layers, share, half), F32),
             pltpu.VMEM((depth, share, half), F32),
-            dma((3,)), dma((layers,)), dma((layers,)), dma((layers,)), dma((layers,)),
+            dma((2,)), dma((layers,)), dma((layers,)), dma((layers,)), dma((layers,)),
             dma((layers,)), dma((layers,)), dma((layers,)), dma((layers,)),
             dma((layers, nz - 1)), dma((layers, nz - 1)), dma((depth,)), dma((depth,)),
         ],
         compiler_params=pltpu.CompilerParams(
-            collective_id=1, has_side_effects=True, vmem_limit_bytes=limit
+            collective_id=0, has_side_effects=True, vmem_limit_bytes=limit
         ),
         name="layers",
-    )(received, dest, resets, w_all, gain_all, decay_all, cot)
+    )(blocks, dest, resets, w_query, gain, decay, cot)
 
 
 def local(blocks, dest, resets, w_query, gain, decay, cot):

time: 68.5 us -> 59.2 us (0.86)
  Pallas kernels: 66.5 us -> 57.3 us
    pallas_call x1 -> x0, Pallas kernels: 16.4 us -> none  [split_batches(): pl.pallas_call(functools.partial(exchange_kernel, groups, slot), out_shap...]
    pallas_call x1, Pallas kernels: 50.1 us -> 57.3 us  [split_batches(): pl.pallas_call(functools.partial(layers_kernel, heads, slot), out_shape=j...]
where the time goes in v3:
time: 59.2 us; the launch traced here: 59 us
  Pallas kernels  57.3 us (97%)
  local copies, waits for them, and re-layouts  1.67 us (3%)
    pallas_call x1, Pallas kernels, split_batches(): pl.pallas_call(functools.partial(layers_kernel, heads, slot), out_shape=j...  57.3 us
    unnamed x1, local copies, waits for them, and re-layouts  1.67 us

profile of v3, /device:TPU:1, one launch (start us, length us, event | category | flops | bytes accessed | tf_op | source)
XLA Modules:
  0.0 59.0 jit_solution(12760255266725379422)
XLA Ops:
  0.0 57.3 %layers.1 = f32[2,64,512]{2,1,0:T(8,128)} custom-call(bf16[2,192,1024]{2,1,0:T(8,128)(2,1)} %blocks_ref.1, s32[2,16,48]{2,1,0:T(8,128)} %dest_ref.1, s32[2,32]{1,0:T(2,128)} %resets_ref.1, bf16[2,1024,512]{2,1,0:T(8,128)(2,1)} %w_own.1, f32[2,1024]{1,0:T(2,128)} %gain_own.1, f32[2,8]{1,0:T(2,128)} %decay_own.1, bf16[2,192,1024]{2,1,0:T(8,128)(2,1)} %cot_ref.1), custom_call_target="tpu_custom_call" | custom-call | tf_op jit(solution)/shard_map/layers/pallas_call | solution.py:544
  57.3 1.7 %copy.9 = f32[2,64,512]{2,1,0:T(8,128)} copy(f32[2,64,512]{2,1,0:T(8,128)} %layers.1) | data formatting | bytes 524288

commit v4 on v3

--- a/solution.py
+++ b/solution.py
@@ -471,8 +471,6 @@
 
     def backward(l):
         for h in range(heads):
-            if h == heads // 2 and l + 1 < layers:
-                weight_part(l + 1)
             cols = slice(h * dv, (h + 1) * dv)
             dn = dy_s[:, cols].astype(F32)
             n = n_s[l, :, cols]
@@ -500,12 +498,12 @@
         l = layers - 1 - step
         if l >= 0:
             backward(l)
-        if l == -1:
-            weight_part(0)
         if 0 <= l + 2 < layers:
-            stage_two(l + 2)
-        if 0 <= l + 3 < layers:
-            stage_three(l + 3)
+            stage_three(l + 2)
+        if 0 <= l + 1 < layers:
+            stage_two(l + 1)
+        if l >= 0:
+            weight_part(l)
         if 0 <= l + 4 < layers:
             finish_sum(l + 4)
 

time: 59.2 us -> 66 us (1.11)
  the two profiles are of different devices: /device:TPU:1 before, /device:TPU:5 now
where the time goes in v4:
time: 66 us; the launch traced here: 65.8 us
  Pallas kernels  64.1 us (97%)
  local copies, waits for them, and re-layouts  1.67 us (3%)
    pallas_call x1, Pallas kernels, split_batches(): pl.pallas_call(functools.partial(layers_kernel, heads, slot), out_shape=j...  64.1 us
    unnamed x1, local copies, waits for them, and re-layouts  1.67 us

profile of v4, /device:TPU:5, one launch (start us, length us, event | category | flops | bytes accessed | tf_op | source)
XLA Modules:
  0.0 65.8 jit_solution(15856075546597171974)
XLA Ops:
  0.0 64.1 %layers.1 = f32[2,64,512]{2,1,0:T(8,128)} custom-call(bf16[2,192,1024]{2,1,0:T(8,128)(2,1)} %blocks_ref.1, s32[2,16,48]{2,1,0:T(8,128)} %dest_ref.1, s32[2,32]{1,0:T(2,128)} %resets_ref.1, bf16[2,1024,512]{2,1,0:T(8,128)(2,1)} %w_own.1, f32[2,1024]{1,0:T(2,128)} %gain_own.1, f32[2,8]{1,0:T(2,128)} %decay_own.1, bf16[2,192,1024]{2,1,0:T(8,128)(2,1)} %cot_ref.1), custom_call_target="tpu_custom_call" | custom-call | tf_op jit(solution)/shard_map/layers/pallas_call | solution.py:542
  64.1 1.7 %copy.9 = f32[2,64,512]{2,1,0:T(8,128)} copy(f32[2,64,512]{2,1,0:T(8,128)} %layers.1) | data formatting | bytes 524288
